TPU v7x, 32 devices: a whole 2x2x4 slice. The times are simulated.
32 devices in a mesh: grp: 2 (over y), box: 4 (over z), lvl: 2 (over x), rhs: 2 (over core).
Axes of the slice: x: 2, y: 2, z: 4, core: 2. Of those that a mesh axis runs over, the one named last changes fastest.
Arguments:
- charges: bfloat16 [64, 16384], P('rhs', ('grp', 'box', 'lvl')), parts along dimension 1, may hold values from -6 to 6
- counts: int32 [256], P(('grp', 'box', 'lvl')), parts along dimension 0, may hold values from 8 to 64
- basis: bfloat16 [256, 64, 64], P(('grp', 'box', 'lvl')), parts along dimension 0, may hold values from -0.75 to 0.75
- transfer: bfloat16 [256, 64, 64], P(('grp', 'box', 'lvl')), parts along dimension 0, may hold values from -0.25 to 0.25
- far_coupling: bfloat16 [256, 20, 64, 64], P(('grp', 'box', 'lvl')), parts along dimension 0, may hold values from -0.15625 to 0.15625
- far_list: int32 [256, 12], P(('grp', 'box', 'lvl')), parts along dimension 0, may hold values from 0 to 127, as said below
- far_slot: int32 [256, 8], P(('grp', 'box', 'lvl')), parts along dimension 0, may hold values from 0 to 7, as said below
- send_rows: int32 [16, 8, 1], P(('grp', 'box', 'lvl')), parts along dimension 0, may hold values from 0 to 15
- coarse_coupling: bfloat16 [32, 4, 64, 64], P(('grp', 'box', 'lvl')), parts along dimension 0, may hold values from -0.375 to 0.375
- near_blocks: bfloat16 [256, 9, 64, 64], P(('grp', 'box', 'lvl')), parts along dimension 0, may hold values from -0.25 to 0.25
- near_list: int32 [256, 9], P(('grp', 'box', 'lvl')), parts along dimension 0, may hold values from 0 to 127, as said below
Outputs:
- potential: bfloat16 [64, 16384], P('rhs', ('grp', 'box', 'lvl')), parts along dimension 1
There are 2 independent parts, one for each index of `grp`. A program takes and returns all parts, laid end to end along the dimension named above; each array names one. Nothing has to cross between parts.
Inputs may be any that keep to these rules, and one draw needn't show every extreme that they name: `near_list`: entries lie within 4 leaf boxes of the row's own leaf box; the first entry of each row is the leaf box itself. `far_list`: entries of row l name leaf boxes held by index l // 16 of box and lvl or by the index just before or after it. `far_slot`: each index's rows name every slot of the 8 it receives.
All inputs are finite; a program needn't handle non-finite values.
Results may differ from a plain program's by a relative error of at most 0.0053.
Values may be sent and summed in bfloat16 or wider, within the bound.
A program may use at most 128 MiB of HBM per device.

v0:
```python
import jax
import jax.numpy as jnp
from jax import lax
from jax.sharding import PartitionSpec as P

HALO = 4


def padded(cells, sides, width):
    for axis, dim in sides:
        count = lax.axis_size(axis)
        ends = count - 1
        head = lax.slice_in_dim(cells, 0, width, axis=dim)
        tail = lax.slice_in_dim(cells, cells.shape[dim] - width, cells.shape[dim], axis=dim)
        cells = jnp.concatenate(
            [
                lax.ppermute(tail, axis, [(i, (i + 1) % count) for i in range(ends)]),
                cells,
                lax.ppermute(head, axis, [((i + 1) % count, i) for i in range(ends)]),
            ],
            axis=dim,
        )
    return cells


def on_device(
    charges,
    counts,
    basis,
    transfer,
    far_coupling,
    far_list,
    far_slot,
    send_rows,
    coarse_coupling,
    near_blocks,
    near_list,
):
    leaf_dev = counts.shape[0]
    points = basis.shape[1]
    rank_width = basis.shape[2]
    columns = charges.shape[0]
    slot_count = send_rows.shape[2]
    win_count = far_list.shape[1]
    parents = leaf_dev // 8
    position = lax.axis_index(("box", "lvl"))
    live = jnp.arange(points)[None, :] < counts[:, None]
    blocks = charges.reshape(columns, leaf_dev, points)
    masked = jnp.where(live[None], blocks, jnp.zeros((), charges.dtype))
    coef = jnp.einsum("lpr,clp->lcr", basis, masked, preferred_element_type=jnp.float32).astype(
        jnp.bfloat16
    )
    tr_groups = transfer.reshape(parents, 8, rank_width, rank_width)
    upward = jnp.einsum(
        "nkrs,nkcr->ncs",
        tr_groups,
        coef.reshape(parents, 8, columns, rank_width),
        preferred_element_type=jnp.float32,
    ).astype(jnp.bfloat16)
    window_coupling = far_coupling[:, :win_count]
    tail_coupling = far_coupling[:, win_count:]
    coef_all = lax.all_gather(coef, ("box", "lvl"), axis=0, tiled=True)
    rows_all = lax.all_gather(send_rows, ("box", "lvl"), axis=0, tiled=True)
    window_part = jnp.einsum(
        "lkrs,lkcs->lcr", window_coupling, coef_all[far_list], preferred_element_type=jnp.float32
    )
    peer = far_slot // slot_count
    within = far_slot % slot_count
    source = peer * leaf_dev + rows_all[peer, position, within]
    tail_part = jnp.einsum(
        "lkrs,lkcs->lcr", tail_coupling, coef_all[source], preferred_element_type=jnp.float32
    )
    farfield = window_part + tail_part
    coarse = jnp.einsum(
        "tsrq,scq->tcr",
        coarse_coupling,
        lax.all_gather(upward, "lvl", axis=0, tiled=True),
        preferred_element_type=jnp.float32,
    ).astype(jnp.bfloat16)
    downward = jnp.einsum(
        "nkrs,ncs->nkcr", tr_groups, coarse, preferred_element_type=jnp.float32
    ).reshape(leaf_dev, columns, rank_width)
    local = (farfield + downward).astype(jnp.bfloat16)
    far_part = jnp.einsum("lpr,lcr->clp", basis, local, preferred_element_type=jnp.float32)
    extended = padded(
        masked.reshape(columns, leaf_dev * points), ((("box", "lvl"), 1),), HALO * points
    )
    extended = extended.reshape(columns, leaf_dev + 2 * HALO, points)
    local_index = near_list - (position * leaf_dev - HALO)
    picked_near = extended[:, local_index]
    near_part = jnp.einsum(
        "ljpq,cljq->clp", near_blocks, picked_near, preferred_element_type=jnp.float32
    )
    total = jnp.where(live[None], near_part + far_part, jnp.zeros((), jnp.float32))
    return total.reshape(columns, leaf_dev * points).astype(jnp.bfloat16)


def solution(mesh):
    placed = (
        P("rhs", ("grp", "box", "lvl")),
        P(("grp", "box", "lvl")),
        P(("grp", "box", "lvl"), None, None),
        P(("grp", "box", "lvl"), None, None),
        P(("grp", "box", "lvl"), None, None, None),
        P(("grp", "box", "lvl"), None),
        P(("grp", "box", "lvl"), None),
        P(("grp", "box", "lvl"), None, None),
        P(("grp", "box", "lvl"), None, None, None),
        P(("grp", "box", "lvl"), None, None, None),
        P(("grp", "box", "lvl"), None),
    )
    return jax.shard_map(
        on_device,
        mesh=mesh,
        in_specs=placed,
        out_specs=P("rhs", ("grp", "box", "lvl")),
        check_vma=False,
    )
```

profile of v0, /device:TPU:0, one launch (start us, length us, event | category | flops | bytes accessed | tf_op | source)
XLA Modules:
  0.0 95.2 jit_solution(1539083016644055399)
XLA Ops:
  0.0 0.0 copy-start
  0.0 0.9 broadcast_reduce_fusion
  0.9 0.1 lt.60
  1.0 0.1 lt.58
  1.1 0.8 broadcast_select_fusion
  1.9 0.6 fusion.36
  2.5 4.8 %collective-permute-start = (bf16[32,256]{1,0:T(8,128)(2,1)}, bf16[32,256]{1,0:T(8,128)(2,1)S(1)}, u32[]{:S(2)}, u32[]{:S(2)}) collective-permute-start(bf16[32,256]{1,0:T(8,128)(2,1)} %get-tuple-element.5), channel_id=1, source_target_pairs={{0,2},{2,4},{4,6},{6,8},{8,10},{10,12},{12,14},{1,3},{3,5},{5,7},{... | collective-permute-start | bytes 49160 | tf_op jit(solution)/shard_map/ppermute | solution.py:17
  7.4 1.3 %collective-permute-start.1 = (bf16[32,256]{1,0:T(8,128)(2,1)}, bf16[32,256]{1,0:T(8,128)(2,1)}, u32[]{:S(2)}, u32[]{:S(2)}) collective-permute-start(bf16[32,256]{1,0:T(8,128)(2,1)} %get-tuple-element.6), channel_id=1, source_target_pairs={{2,0},{4,2},{6,4},{8,6},{10,8},{12,10},{14,12},{3,1},{5,3},{7,5},{... | collective-permute-start | bytes 49160 | tf_op jit(solution)/shard_map/ppermute | solution.py:19
  8.7 0.7 iota_compare_fusion
  9.4 1.0 %reshape.42 = bf16[32,16,64]{2,1,0:T(8,128)(2,1)S(1)} reshape(bf16[32,1024]{1,0:T(8,128)(2,1)} %param.11) | data formatting | bytes 131072 | tf_op jit(solution)/shard_map/reshape | solution.py:48
  10.4 22.6 %all_gather.10 = s32[8,8,1]{1,2,0:T(1,128)S(1)} all-gather(s32[1,8,1]{1,2,0:T(1,128)} %param.18), channel_id=1, replica_groups=mesh['grp'=2,'box'=4,'lvl'=2,'rhs'=2] {'box','lvl'}, dimensions={0}, use_global_device_ids=true | all-gather | bytes 288 | tf_op jit(solution)/shard_map/all_gather | solution.py:63
  33.0 0.7 compare_select_fusion.3
  33.7 0.1 reshape.48
  33.8 0.8 copy.40
  34.6 0.1 reshape.62
  34.7 0.0 copy-start.5
  34.7 0.0 copy-start.1
  34.7 1.4 %gather_fusion.2 = s32[128]{0:T(128)S(1)} fusion(s32[8,8,1]{1,2,0:T(1,128)S(1)} %all_gather.10, s32[128]{0:T(128)S(1)} %reshape.62), kind=kCustom, calls=%fused_computation.2 | custom fusion | bytes 2560 | tf_op jit(solution)/shard_map/gather | solution.py:69
  36.1 0.1 reshape.65
  36.2 0.1 reshape.70
  36.3 0.0 copy-done.5
  36.3 0.1 reshape.56
  36.4 0.0 copy-done.1
  36.4 0.2 convolution_convert_fusion
  36.6 34.5 %all_gather.9 = bf16[128,32,64]{2,1,0:T(8,128)(2,1)S(1)} all-gather(bf16[16,32,64]{2,1,0:T(8,128)(2,1)S(1)} %convolution_convert_fusion), channel_id=1, replica_groups=mesh['grp'=2,'box'=4,'lvl'=2,'rhs'=2] {'box','lvl'}, dimensions={0}, use_global_device_ids=true | all-gather | bytes 589824 | tf_op jit(solution)/shard_map/all_gather | solution.py:62
  71.1 1.2 %fusion.22 = bf16[2,32,64]{2,1,0:T(8,128)(2,1)S(1)} fusion(bf16[2,8,32,64]{3,2,1,0:T(8,128)(2,1)S(1)} %bitcast.68, bf16[2,8,64,64]{3,2,1,0:T(8,128)(2,1)} %bitcast.69), kind=kOutput, calls=%fused_computation.21 | convolution fusion | flops 4198400 | bytes 204800 | tf_op jit(solution)/shard_map/nkrs,nkcr->ncs/dot_general | solution.py:54
  72.3 4.4 %all_gather.11 = bf16[4,32,64]{2,1,0:T(8,128)(2,1)S(1)} all-gather(bf16[2,32,64]{2,1,0:T(8,128)(2,1)S(1)} %fusion.22), channel_id=1, replica_groups=mesh['grp'=2,'box'=4,'lvl'=2,'rhs'=2] {'lvl'}, dimensions={0}, use_global_device_ids=true | all-gather | bytes 24576 | tf_op jit(solution)/shard_map/all_gather | solution.py:77
  76.7 2.3 %fusion.27 = f32[2,32,8,64]{3,1,2,0:T(8,128)} fusion(bf16[2,8,64,64]{3,2,1,0:T(8,128)(2,1)} %bitcast.70, bf16[2,4,64,64]{3,2,1,0:T(8,128)(2,1)} %param.19, bf16[4,32,64]{2,1,0:T(8,128)(2,1)S(1)} %all_gather.11), kind=kOutput, calls=%fused_computation.24 | convolution fusion | flops 6295552 | bytes 344064 | tf_op jit(solution)/shard_map/nkrs,ncs->nkcr/dot_general | solution.py:80
  79.0 1.7 %gather_fusion.3 = bf16[128,32,64]{2,1,0:T(8,128)(2,1)} fusion(bf16[128,32,64]{2,1,0:T(8,128)(2,1)S(1)} %all_gather.9, s32[1024]{0:T(1024)S(1)} %pad_clamp_fusion), kind=kCustom, calls=%fused_computation.3 | custom fusion | bytes 1049088 | tf_op jit(solution)/shard_map/gather | solution.py:71
  80.6 3.3 %fusion.8 = f32[16,32,64]{2,1,0:T(8,128)} fusion(bf16[16,8,32,64]{3,2,1,0:T(8,128)(2,1)} %bitcast.67, bf16[16,20,64,64]{3,2,1,0:T(8,128)(2,1)} %param.15), kind=kOutput, calls=%fused_computation.11 | convolution fusion | flops 33554432 | bytes 3276800 | tf_op jit(solution)/shard_map/lkrs,lkcs->lcr/dot_general | solution.py:70
  83.9 2.0 %gather_fusion.1 = bf16[192,32,64]{2,1,0:T(8,128)(2,1)} fusion(bf16[128,32,64]{2,1,0:T(8,128)(2,1)S(1)} %all_gather.9, s32[1024]{0:T(1024)S(1)} %pad_clamp_fusion.1), kind=kCustom, calls=%fused_computation.1 | custom fusion | bytes 1573632 | tf_op jit(solution)/shard_map/gather | solution.py:65
  85.9 0.0 collective-permute-done
  85.9 0.0 collective-permute-done.1
  85.9 0.7 pad_maximum_fusion
  86.7 0.2 reshape.41
  86.9 1.8 %gather_fusion = bf16[144,32,64]{2,1,0:T(8,128)(2,1)} fusion(bf16[32,24,64]{2,0,1:T(8,128)(2,1)S(1)} %copy.38, s32[1024]{0:T(1024)S(1)} %pad_clamp_fusion.2), kind=kCustom, calls=%fused_computation | custom fusion | bytes 1180224 | tf_op jit(solution)/shard_map/gather | solution.py:90
  88.7 0.0 copy-start.2
  88.7 0.0 copy-start.3
  88.7 0.0 copy-start.4
  88.7 0.0 copy-done
  88.7 2.1 %convolution_bitcast_fusion = f32[16,32,64]{2,1,0:T(8,128)S(1)} fusion(bf16[32,16,9,64]{3,0,2,1:T(8,128)(2,1)} %bitcast.65, bf16[16,9,64,64]{3,2,1,0:T(8,128)(2,1)S(1)} %copy-done), kind=kOutput, calls=%fused_computation.12 | convolution fusion | flops 37748736 | bytes 1900544 | tf_op jit(solution)/shard_map/ljpq,cljq->clp/dot_general | solution.py:91
  90.9 0.0 copy-done.2
  90.9 0.0 copy-done.3
  90.9 0.0 copy-done.4
  90.9 3.4 %fusion.21 = bf16[32,16,64]{2,0,1:T(8,128)(2,1)S(1)} fusion(f32[16,32,64]{2,1,0:T(8,128)S(1)} %convolution_bitcast_fusion, bf16[16,64,64]{2,1,0:T(8,128)(2,1)S(1)} %copy-done.2, f32[16,32,64]{2,1,0:T(8,128)S(1)} %bitcast.71, f32[16,32,64]{2,1,0:T(8,128)S(1)} %copy-done.4, bf16[16,12,32,64]{3,2,1,0:T(8,128)(2,1)} %bitcast.66, ...), kind=kOutput, calls=%fused_computation.18 | convolution fusion | flops 54722560 | bytes 5309440 | tf_op jit(solution)/shard_map/lpr,lcr->clp/dot_general | solution.py:84
  94.3 0.1 copy.44
  94.4 0.8 convert_element_type.31
  (9 shorter events, 0.1 us)
Async XLA Ops:
  0.0 88.7 %copy-start = (bf16[16,9,64,64]{3,2,1,0:T(8,128)(2,1)S(1)}, bf16[16,9,64,64]{3,2,1,0:T(8,128)(2,1)}, u32[]{:S(2)}) copy-start(bf16[16,9,64,64]{3,2,1,0:T(8,128)(2,1)} %param.20) | copy-start | bytes 3538948
  2.5 83.4 %collective-permute-start = (bf16[32,256]{1,0:T(8,128)(2,1)}, bf16[32,256]{1,0:T(8,128)(2,1)S(1)}, u32[]{:S(2)}, u32[]{:S(2)}) collective-permute-start(bf16[32,256]{1,0:T(8,128)(2,1)} %get-tuple-element.5), channel_id=1, source_target_pairs={{0,2},{2,4},{4,6},{6,8},{8,10},{10,12},{12,14},{1,3},{3,5},{5,7},{... | collective-permute-start | bytes 49160 | tf_op jit(solution)/shard_map/ppermute | solution.py:17
  7.4 78.6 %collective-permute-start.1 = (bf16[32,256]{1,0:T(8,128)(2,1)}, bf16[32,256]{1,0:T(8,128)(2,1)}, u32[]{:S(2)}, u32[]{:S(2)}) collective-permute-start(bf16[32,256]{1,0:T(8,128)(2,1)} %get-tuple-element.6), channel_id=1, source_target_pairs={{2,0},{4,2},{6,4},{8,6},{10,8},{12,10},{14,12},{3,1},{5,3},{7,5},{... | collective-permute-start | bytes 49160 | tf_op jit(solution)/shard_map/ppermute | solution.py:19
  34.7 1.6 %copy-start.5 = (s32[16,12]{1,0:T(8,128)S(1)}, s32[16,12]{1,0:T(8,128)}, u32[]{:S(2)}) copy-start(s32[16,12]{1,0:T(8,128)} %param.16) | copy-start | bytes 2308
  34.7 1.7 %copy-start.1 = (bf16[16,64,64]{2,1,0:T(8,128)(2,1)S(1)}, bf16[16,64,64]{2,1,0:T(8,128)(2,1)}, u32[]{:S(2)}) copy-start(bf16[16,64,64]{2,1,0:T(8,128)(2,1)} %param.13) | copy-start | bytes 393220
  88.7 2.2 %copy-start.2 = (bf16[16,64,64]{2,1,0:T(8,128)(2,1)S(1)}, bf16[16,64,64]{2,1,0:T(8,128)(2,1)}, u32[]{:S(2)}) copy-start(bf16[16,64,64]{2,1,0:T(8,128)(2,1)} %param.13) | copy-start | bytes 393220
  88.7 2.2 %copy-start.3 = (f32[2,32,8,64]{3,1,2,0:T(8,128)S(1)}, f32[2,32,8,64]{3,1,2,0:T(8,128)}, u32[]{:S(2)}) copy-start(f32[2,32,8,64]{3,1,2,0:T(8,128)} %fusion.27) | copy-start | bytes 393220
  88.7 2.2 %copy-start.4 = (f32[16,32,64]{2,1,0:T(8,128)S(1)}, f32[16,32,64]{2,1,0:T(8,128)}, u32[]{:S(2)}) copy-start(f32[16,32,64]{2,1,0:T(8,128)} %fusion.8) | copy-start | bytes 393220
where the time goes:
time: 95.7 us; the launch traced here: 95.2 us
  blocking collectives  61.5 us (64%)
  matrix products  12.5 us (13%)
  local copies, waits for them, and re-layouts  11.8 us (12%)
  starting transfers between devices  6.12 us (6%)
  other arithmetic  3.06 us (3%)
    all_gather x1, blocking collectives, on_device(): coef_all = lax.all_gather(coef, ('box', 'lvl'), axis=0, tiled=True)  34.5 us
    all_gather x1, blocking collectives, on_device(): rows_all = lax.all_gather(send_rows, ('box', 'lvl'), axis=0, tiled=True)  22.6 us
    ppermute x1, starting transfers between devices, padded(): lax.ppermute(tail, axis, [(i, (i + 1) % count) for i in range(ends)])  4.83 us
    all_gather x1, blocking collectives, on_device(): lax.all_gather(upward, 'lvl', axis=0, tiled=True)  4.42 us
    dot_general x1, matrix products, on_device(): jnp.einsum('lpr,lcr->clp', basis, local, preferred_element_type=jnp.float32)  3.44 us
    dot_general x1, matrix products, on_device(): jnp.einsum('lkrs,lkcs->lcr', tail_coupling, coef_all[source], preferred_e...  3.31 us
    dot_general x1, matrix products, on_device(): jnp.einsum('nkrs,ncs->nkcr', tr_groups, coarse, preferred_element_type=jn...  2.29 us
    dot_general x1, matrix products, on_device(): jnp.einsum('ljpq,cljq->clp', near_blocks, picked_near, preferred_element_...  2.13 us
  transfers between devices with their start and end apart: 2, of which 0 were waited for; matrix products, arithmetic and copies ran while one was open for 16% of the time, Pallas kernels for 0%

commit v1 on v0

v1 whole, which is shorter than its diff:
```python
import functools

import jax
import jax.numpy as jnp
from jax import lax
from jax.experimental import pallas as pl
from jax.experimental.pallas import tpu as pltpu
from jax.sharding import PartitionSpec as P

HALO = 4
FAMILY = 8
MESH = pl.DeviceIdType.MESH
UNROLL = 1


def nn(a, b):
    return lax.dot_general(a, b, (((1,), (0,)), ((), ())), preferred_element_type=jnp.float32)


def nt(a, b):
    return lax.dot_general(a, b, (((1,), (1,)), ((), ())), preferred_element_type=jnp.float32)


def kernel(
    lvl_count,
    index_count,
    charges_hbm,
    counts_hbm,
    basis_hbm,
    transfer_hbm,
    far_hbm,
    far_list_hbm,
    far_slot_hbm,
    rows_hbm,
    coarse_hbm,
    near_hbm,
    near_list_hbm,
    out_ref,
    charges,
    basis,
    transfer,
    far,
    coupling,
    near,
    counts,
    far_list,
    far_slot,
    rows,
    near_list,
    cells,
    own,
    window,
    stage,
    tail,
    up_own,
    up_all,
    coarse,
    near_sum,
    load_sem,
    halo_send,
    halo_recv,
    win_send,
    win_recv,
    tail_send,
    tail_recv,
    up_send,
    up_recv,
):
    box = lax.axis_index("box")
    lvl = lax.axis_index("lvl")
    me = box * lvl_count + lvl
    leaf_dev, points, rank = basis.shape
    win_count = far_list.shape[1]
    tail_count = far_slot.shape[0]
    near_count = near.shape[1]
    cap = rows.shape[1]
    parents = up_own.shape[0]
    group = coupling.shape[1]
    wide = 2 * points
    cell_ring = cells.shape[0]
    win_ring = window.shape[0]
    cell_home = lax.rem(me, 2) * leaf_dev
    win_home = lax.rem(me, win_ring // leaf_dev) * leaf_dev

    loads = [
        pltpu.make_async_copy(source, target, load_sem.at[i])
        for i, (source, target) in enumerate(
            (
                (charges_hbm, charges),
                (counts_hbm, counts),
                (basis_hbm, basis),
                (rows_hbm, rows),
                (transfer_hbm, transfer),
                (near_list_hbm, near_list),
                (near_hbm, near),
                (coarse_hbm, coupling),
                (far_list_hbm, far_list),
                (far_slot_hbm, far_slot),
                (far_hbm, far),
            )
        )
    ]
    for load in loads:
        load.start()

    def place(index):
        return {"box": lax.div(index, lvl_count), "lvl": lax.rem(index, lvl_count)}

    def other(step):
        return lax.rem(me + step, index_count)

    barrier = pltpu.get_barrier_semaphore()

    @pl.loop(1, index_count)
    def _(step):
        pl.semaphore_signal(barrier, inc=1, device_id=place(other(step)), device_id_type=MESH)

    has_prev = me > 0
    has_next = me < index_count - 1
    prev_place = place(lax.max(me - 1, 0))
    next_place = place(lax.min(me + 1, index_count - 1))

    def remote(source, target, send, recv, where):
        return pltpu.make_async_remote_copy(
            src_ref=source,
            dst_ref=target,
            send_sem=send,
            recv_sem=recv,
            device_id=where,
            device_id_type=MESH,
        )

    halo_next = remote(
        cells.at[pl.ds(cell_home + leaf_dev - HALO, HALO)],
        cells.at[pl.ds(cell_home + leaf_dev - HALO, HALO)],
        halo_send.at[0],
        halo_recv.at[0],
        next_place,
    )
    halo_prev = remote(
        cells.at[pl.ds(cell_home, HALO)],
        cells.at[pl.ds(cell_home, HALO)],
        halo_send.at[1],
        halo_recv.at[1],
        prev_place,
    )
    win_next = remote(own, window.at[pl.ds(win_home, leaf_dev)], win_send.at[0], win_recv.at[0], next_place)
    win_prev = remote(own, window.at[pl.ds(win_home, leaf_dev)], win_send.at[1], win_recv.at[1], prev_place)

    def tail_copy(step):
        peer = other(step)
        return remote(
            stage.at[pl.ds(peer * cap, cap)],
            tail.at[pl.ds(me * cap, cap)],
            tail_send.at[step],
            tail_recv.at[step],
            place(peer),
        )

    def up_copy(step):
        return remote(
            up_own,
            up_all.at[pl.ds(lvl * parents, parents)],
            up_send.at[step],
            up_recv.at[step],
            {"lvl": lax.rem(lvl + step, lvl_count)},
        )

    lanes = lax.broadcasted_iota(jnp.int32, (charges.shape[0], wide), 1)

    def live(pair):
        first = counts[2 * pair]
        second = counts[2 * pair + 1] + points
        return (lanes < first) | ((lanes >= points) & (lanes < second))

    loads[0].wait()
    loads[1].wait()

    for pair in range(leaf_dev // 2):
        block = charges[:, pair * wide : (pair + 1) * wide]
        block = jnp.where(live(pair), block.astype(jnp.float32), 0.0).astype(jnp.bfloat16)
        cells[cell_home + 2 * pair] = block[:, :points]
        cells[cell_home + 2 * pair + 1] = block[:, points:]

    pl.semaphore_wait(barrier, index_count - 1)

    @pl.when(has_next)
    def _():
        halo_next.start()

    @pl.when(has_prev)
    def _():
        halo_prev.start()

    loads[2].wait()

    for leaf in range(leaf_dev):
        value = nn(cells[cell_home + leaf], basis[leaf]).astype(jnp.bfloat16)
        own[leaf] = value
        window[win_home + leaf] = value

    @pl.when(has_next)
    def _():
        win_next.start()

    @pl.when(has_prev)
    def _():
        win_prev.start()

    loads[3].wait()

    @pl.loop(1, index_count)
    def _(step):
        peer = other(step)
        for j in range(cap):
            stage[peer * cap + j] = own[rows[0, j, peer]]
        tail_copy(step).start()

    for j in range(cap):
        tail[me * cap + j] = own[rows[0, j, me]]

    loads[4].wait()
    for parent in range(parents):
        total = None
        for k in range(FAMILY):
            leaf = parent * FAMILY + k
            term = nn(own[leaf], transfer[leaf])
            total = term if total is None else total + term
        value = total.astype(jnp.bfloat16)
        up_own[parent] = value
        up_all[lvl * parents + parent] = value

    @pl.loop(1, lvl_count)
    def _(step):
        up_copy(step).start()

    loads[5].wait()
    loads[6].wait()

    @pl.when(has_prev)
    def _():
        halo_next.wait_recv()

    @pl.when(has_next)
    def _():
        halo_prev.wait_recv()

    def near_body(pair, _):
        sums = []
        for half in range(2):
            leaf = 2 * pair + half
            total = None
            for k in range(near_count):
                source = near_list[leaf, k] & (cell_ring - 1)
                term = nt(cells[source], near[leaf, k])
                total = term if total is None else total + term
            sums.append(total)
        near_sum[pair] = jnp.concatenate(sums, axis=1)
        return _

    lax.fori_loop(0, leaf_dev // 2, near_body, 0, unroll=UNROLL)

    loads[7].wait()

    @pl.loop(1, lvl_count)
    def _(step):
        up_copy(step).wait_recv()

    for parent in range(parents):
        total = None
        for k in range(group):
            term = nt(up_all[k], coupling[parent, k])
            total = term if total is None else total + term
        coarse[parent] = total.astype(jnp.bfloat16)

    loads[8].wait()
    loads[9].wait()
    loads[10].wait()

    @pl.when(has_prev)
    def _():
        win_next.wait_recv()

    @pl.when(has_next)
    def _():
        win_prev.wait_recv()

    @pl.loop(1, index_count)
    def _(step):
        tail_copy(step).wait_recv()

    def far_body(pair, _):
        parts = []
        for half in range(2):
            leaf = 2 * pair + half
            total = nt(coarse[lax.div(pair, FAMILY // 2)], transfer[leaf])
            for k in range(win_count):
                source = far_list[leaf, k] & (win_ring - 1)
                total = total + nt(window[source], far[leaf, k])
            for k in range(tail_count):
                total = total + nt(tail[far_slot[k, leaf]], far[leaf, win_count + k])
            parts.append(nt(total.astype(jnp.bfloat16), basis[leaf]))
        total = near_sum[pair] + jnp.concatenate(parts, axis=1)
        total = jnp.where(live(pair), total, 0.0)
        out_ref[:, pl.ds(pl.multiple_of(pair * wide, wide), wide)] = total.astype(jnp.bfloat16)
        return _

    lax.fori_loop(0, leaf_dev // 2, far_body, 0, unroll=UNROLL)

    @pl.when(has_next)
    def _():
        halo_next.wait_send()
        win_next.wait_send()

    @pl.when(has_prev)
    def _():
        halo_prev.wait_send()
        win_prev.wait_send()

    @pl.loop(1, index_count)
    def _(step):
        tail_copy(step).wait_send()

    @pl.loop(1, lvl_count)
    def _(step):
        up_copy(step).wait_send()


def on_device(
    lvl_count,
    index_count,
    charges,
    counts,
    basis,
    transfer,
    far_coupling,
    far_list,
    far_slot,
    send_rows,
    coarse_coupling,
    near_blocks,
    near_list,
):
    columns = charges.shape[0]
    leaf_dev, points, rank = basis.shape
    parents, group = coarse_coupling.shape[:2]
    cap = send_rows.shape[2]
    far_slot = far_slot.T
    send_rows = send_rows.transpose(0, 2, 1)
    half = jnp.bfloat16

    def cell(count):
        return pltpu.VMEM((count, columns, rank), half)

    dma = pltpu.SemaphoreType.DMA
    return pl.pallas_call(
        functools.partial(kernel, lvl_count, index_count),
        out_shape=jax.ShapeDtypeStruct(charges.shape, half),
        in_specs=[pl.BlockSpec(memory_space=pl.ANY)] * 11,
        out_specs=pl.BlockSpec(memory_space=pltpu.VMEM),
        scratch_shapes=[
            pltpu.VMEM(charges.shape, half),
            pltpu.VMEM(basis.shape, half),
            pltpu.VMEM(transfer.shape, half),
            pltpu.VMEM(far_coupling.shape, half),
            pltpu.VMEM(coarse_coupling.shape, half),
            pltpu.VMEM(near_blocks.shape, half),
            pltpu.SMEM(counts.shape, jnp.int32),
            pltpu.SMEM(far_list.shape, jnp.int32),
            pltpu.SMEM(far_slot.shape, jnp.int32),
            pltpu.SMEM(send_rows.shape, jnp.int32),
            pltpu.SMEM(near_list.shape, jnp.int32),
            cell(2 * leaf_dev),
            cell(leaf_dev),
            cell(4 * leaf_dev),
            cell(index_count * cap),
            cell(index_count * cap),
            cell(parents),
            cell(group),
            cell(parents),
            pltpu.VMEM((leaf_dev // 2, columns, 2 * points), jnp.float32),
            dma((11,)),
            dma((2,)),
            dma((2,)),
            dma((2,)),
            dma((2,)),
            dma((index_count,)),
            dma((index_count,)),
            dma((lvl_count,)),
            dma((lvl_count,)),
        ],
        compiler_params=pltpu.CompilerParams(
            collective_id=0, has_side_effects=True, vmem_limit_bytes=48 * 1024 * 1024
        ),
    )(
        charges,
        counts,
        basis,
        transfer,
        far_coupling,
        far_list,
        far_slot,
        send_rows,
        coarse_coupling,
        near_blocks,
        near_list,
    )


def solution(mesh):
    every = ("grp", "box", "lvl")
    placed = (
        P("rhs", every),
        P(every),
        P(every, None, None),
        P(every, None, None),
        P(every, None, None, None),
        P(every, None),
        P(every, None),
        P(every, None, None),
        P(every, None, None, None),
        P(every, None, None, None),
        P(every, None),
    )
    lvl_count = mesh.shape["lvl"]
    return jax.shard_map(
        functools.partial(on_device, lvl_count, lvl_count * mesh.shape["box"]),
        mesh=mesh,
        in_specs=placed,
        out_specs=P("rhs", every),
        check_vma=False,
    )
```

time: 95.7 us -> 33.5 us (0.35)
  the two profiles are of different devices: /device:TPU:0 before, /device:TPU:7 now
where the time goes in v1:
time: 33.5 us; the launch traced here: 33.1 us
  Pallas kernels  23.8 us (71%)
  local copies, waits for them, and re-layouts  9.33 us (28%)
    pallas_call x1, Pallas kernels, on_device(): pl.pallas_call(functools.partial(kernel, lvl_count, index_count), out_sha...  23.8 us
    unnamed x21, local copies, waits for them, and re-layouts  9.33 us

profile of v1, /device:TPU:7, one launch (start us, length us, event | category | flops | bytes accessed | tf_op | source)
XLA Modules:
  0.0 33.1 jit_solution(6410818431220372838)
XLA Ops:
  0.0 0.0 copy-start
  0.0 1.7 %copy-done = bf16[16,9,64,64]{3,2,1,0:T(8,128)(2,1)S(1)} copy-done((bf16[16,9,64,64]{3,2,1,0:T(8,128)(2,1)S(1)}, bf16[16,9,64,64]{3,2,1,0:T(8,128)(2,1)}, u32[]{:S(2)}) %copy-start) | copy-done | bytes 1179672
  1.7 0.0 copy-start.1
  1.7 0.9 %copy-done.1 = bf16[16,64,64]{2,1,0:T(8,128)(2,1)S(1)} copy-done((bf16[16,64,64]{2,1,0:T(8,128)(2,1)S(1)}, bf16[16,64,64]{2,1,0:T(8,128)(2,1)}, u32[]{:S(2)}) %copy-start.1) | copy-done | bytes 131096
  2.6 0.0 copy-start.2
  2.6 0.9 %copy-done.2 = bf16[16,64,64]{2,1,0:T(8,128)(2,1)S(1)} copy-done((bf16[16,64,64]{2,1,0:T(8,128)(2,1)S(1)}, bf16[16,64,64]{2,1,0:T(8,128)(2,1)}, u32[]{:S(2)}) %copy-start.2) | copy-done | bytes 131096
  3.6 0.0 copy-start.3
  3.6 0.9 %copy-done.3 = bf16[2,4,64,64]{3,2,1,0:T(8,128)(2,1)S(1)} copy-done((bf16[2,4,64,64]{3,2,1,0:T(8,128)(2,1)S(1)}, bf16[2,4,64,64]{3,2,1,0:T(8,128)(2,1)}, u32[]{:S(2)}) %copy-start.3) | copy-done | bytes 65560
  4.5 0.0 copy-start.4
  4.5 0.8 %copy-done.4 = bf16[32,1024]{1,0:T(8,128)(2,1)S(1)} copy-done((bf16[32,1024]{1,0:T(8,128)(2,1)S(1)}, bf16[32,1024]{1,0:T(8,128)(2,1)}, u32[]{:S(2)}) %copy-start.4) | copy-done | bytes 65560
  5.3 0.0 copy-start.5
  5.3 0.7 %copy-done.5 = s32[16,12]{1,0:T(8,128)S(1)} copy-done((s32[16,12]{1,0:T(8,128)S(1)}, s32[16,12]{1,0:T(8,128)}, u32[]{:S(2)}) %copy-start.5) | copy-done | bytes 792
  6.0 0.0 copy-start.6
  6.0 0.7 %copy-done.6 = s32[16,9]{1,0:T(8,128)S(1)} copy-done((s32[16,9]{1,0:T(8,128)S(1)}, s32[16,9]{1,0:T(8,128)}, u32[]{:S(2)}) %copy-start.6) | copy-done | bytes 600
  6.7 0.0 copy-start.7
  6.7 0.7 %copy-done.7 = s32[16,8]{0,1:T(8,128)S(1)} copy-done((s32[16,8]{0,1:T(8,128)S(1)}, s32[16,8]{0,1:T(8,128)}, u32[]{:S(2)}) %copy-start.7) | copy-done | bytes 536
  7.4 0.0 copy-start.8
  7.4 0.7 %copy-done.8 = s32[16]{0:T(128)S(1)} copy-done((s32[16]{0:T(128)S(1)}, s32[16]{0:T(128)}, u32[]{:S(2)}) %copy-start.8) | copy-done | bytes 88
  8.1 0.0 copy-start.9
  8.1 0.7 %copy-done.9 = s32[1,8,1]{1,2,0:T(1,128)S(1)} copy-done((s32[1,8,1]{1,2,0:T(1,128)S(1)}, s32[1,8,1]{1,2,0:T(1,128)}, u32[]{:S(2)}) %copy-start.9) | copy-done | bytes 56
  8.7 23.8 %shard_map.109 = bf16[32,1024]{1,0:T(8,128)(2,1)S(1)} custom-call(bf16[32,1024]{1,0:T(8,128)(2,1)S(1)} %copy-done.4, s32[16]{0:T(128)S(1)} %copy-done.8, bf16[16,64,64]{2,1,0:T(8,128)(2,1)S(1)} %copy-done.1, bf16[16,64,64]{2,1,0:T(8,128)(2,1)S(1)} %copy-done.2, bf16[16,20,64,64]{3,2,1,0:T(8,128)(2,1)} %far_hbm.1, s32[16,12]{1,0:T(8,128)S(1)} %copy-done.5, ...), custom_call_target="tpu_custom_call" | custom-call | tf_op jit(solution)/shard_map/pallas_call | solution.py:356
  32.5 0.6 %copy.13 = bf16[32,1024]{1,0:T(8,128)(2,1)} copy(bf16[32,1024]{1,0:T(8,128)(2,1)S(1)} %shard_map.109) | data formatting | bytes 131072
Async XLA Ops:
  0.0 1.7 %copy-start = (bf16[16,9,64,64]{3,2,1,0:T(8,128)(2,1)S(1)}, bf16[16,9,64,64]{3,2,1,0:T(8,128)(2,1)}, u32[]{:S(2)}) copy-start(bf16[16,9,64,64]{3,2,1,0:T(8,128)(2,1)} %near_hbm.1) | copy-start | bytes 3538948
  1.7 0.9 %copy-start.1 = (bf16[16,64,64]{2,1,0:T(8,128)(2,1)S(1)}, bf16[16,64,64]{2,1,0:T(8,128)(2,1)}, u32[]{:S(2)}) copy-start(bf16[16,64,64]{2,1,0:T(8,128)(2,1)} %basis_hbm.1) | copy-start | bytes 393220
  2.6 0.9 %copy-start.2 = (bf16[16,64,64]{2,1,0:T(8,128)(2,1)S(1)}, bf16[16,64,64]{2,1,0:T(8,128)(2,1)}, u32[]{:S(2)}) copy-start(bf16[16,64,64]{2,1,0:T(8,128)(2,1)} %transfer_hbm.1) | copy-start | bytes 393220
  3.6 0.9 %copy-start.3 = (bf16[2,4,64,64]{3,2,1,0:T(8,128)(2,1)S(1)}, bf16[2,4,64,64]{3,2,1,0:T(8,128)(2,1)}, u32[]{:S(2)}) copy-start(bf16[2,4,64,64]{3,2,1,0:T(8,128)(2,1)} %coarse_hbm.1) | copy-start | bytes 196612
  4.5 0.8 %copy-start.4 = (bf16[32,1024]{1,0:T(8,128)(2,1)S(1)}, bf16[32,1024]{1,0:T(8,128)(2,1)}, u32[]{:S(2)}) copy-start(bf16[32,1024]{1,0:T(8,128)(2,1)} %charges_hbm.1) | copy-start | bytes 196612
  5.3 0.7 %copy-start.5 = (s32[16,12]{1,0:T(8,128)S(1)}, s32[16,12]{1,0:T(8,128)}, u32[]{:S(2)}) copy-start(s32[16,12]{1,0:T(8,128)} %far_list_hbm.1) | copy-start | bytes 2308
  6.0 0.7 %copy-start.6 = (s32[16,9]{1,0:T(8,128)S(1)}, s32[16,9]{1,0:T(8,128)}, u32[]{:S(2)}) copy-start(s32[16,9]{1,0:T(8,128)} %near_list_hbm.1) | copy-start | bytes 1732
  6.7 0.7 %copy-start.7 = (s32[16,8]{0,1:T(8,128)S(1)}, s32[16,8]{0,1:T(8,128)}, u32[]{:S(2)}) copy-start(s32[16,8]{0,1:T(8,128)} %param.17) | copy-start | bytes 1540
  7.4 0.7 %copy-start.8 = (s32[16]{0:T(128)S(1)}, s32[16]{0:T(128)}, u32[]{:S(2)}) copy-start(s32[16]{0:T(128)} %counts_hbm.1) | copy-start | bytes 196
  8.1 0.7 %copy-start.9 = (s32[1,8,1]{1,2,0:T(1,128)S(1)}, s32[1,8,1]{1,2,0:T(1,128)}, u32[]{:S(2)}) copy-start(s32[1,8,1]{1,2,0:T(1,128)} %param.18) | copy-start | bytes 100

commit v2 on v1

v2 whole, which is shorter than its diff:
```python
import functools

import jax
import jax.numpy as jnp
from jax import lax
from jax.experimental import pallas as pl
from jax.experimental.pallas import tpu as pltpu
from jax.sharding import PartitionSpec as P

HALO = 4
FAMILY = 8
MESH = pl.DeviceIdType.MESH


def nn(a, b):
    return lax.dot_general(a, b, (((1,), (0,)), ((), ())), preferred_element_type=jnp.float32)


def packed(blocks):
    return jnp.concatenate(blocks, axis=1)


def stacked(blocks):
    return jnp.concatenate(blocks, axis=0)


def kernel(
    lvl_count,
    index_count,
    charges_hbm,
    counts_hbm,
    basis_hbm,
    transfer_hbm,
    far_hbm,
    far_list_hbm,
    far_slot_hbm,
    rows_hbm,
    coarse_hbm,
    near_hbm,
    near_list_hbm,
    out_ref,
    charges,
    basis,
    transfer,
    far,
    coupling,
    near,
    counts,
    far_list,
    far_slot,
    rows,
    near_list,
    masked,
    halo,
    own,
    own_flat,
    stage,
    arrived,
    tail_in,
    up_own,
    up_in,
    cells,
    window,
    tail,
    up_all,
    coarse,
    far_packed,
    near_packed,
    near_sum,
    load_sem,
    halo_send,
    halo_recv,
    win_send,
    win_recv,
    tail_send,
    tail_recv,
    up_send,
    up_recv,
):
    box = lax.axis_index("box")
    lvl = lax.axis_index("lvl")
    me = box * lvl_count + lvl
    leaf_dev, points, rank = basis.shape
    columns = charges.shape[0]
    pairs = leaf_dev // 2
    edge = HALO // 2
    far_count = far.shape[1]
    win_count = far_list.shape[1]
    near_count = near.shape[1]
    near_even = near_count // 2 * 2
    cap = rows.shape[1]
    parents = coarse.shape[0]
    group = coupling.shape[1]
    wide = 2 * points
    cell_ring = cells.shape[0]
    win_ring = window.shape[0]
    cell_home = lax.rem(me, 2) * leaf_dev
    cell_away = leaf_dev - cell_home
    blocks = win_ring // leaf_dev
    win_home = lax.rem(me, blocks) * leaf_dev
    win_prev_home = lax.rem(me + blocks - 1, blocks) * leaf_dev
    win_next_home = lax.rem(me + 1, blocks) * leaf_dev

    loads = {}
    for i, (source, target) in enumerate(
        (
            (charges_hbm, charges),
            (counts_hbm, counts),
            (basis_hbm, basis),
            (rows_hbm, rows),
            (transfer_hbm, transfer),
            (near_list_hbm, near_list),
            (near_hbm, near),
            (coarse_hbm, coupling),
            (far_list_hbm, far_list),
            (far_slot_hbm, far_slot),
            (far_hbm, far),
        )
    ):
        loads[i] = pltpu.make_async_copy(source, target, load_sem.at[i])
        loads[i].start()

    def place(index):
        return {"box": lax.div(index, lvl_count), "lvl": lax.rem(index, lvl_count)}

    def other(step):
        return lax.rem(me + step, index_count)

    barrier = pltpu.get_barrier_semaphore()

    @pl.loop(1, index_count)
    def _(step):
        pl.semaphore_signal(barrier, inc=1, device_id=place(other(step)), device_id_type=MESH)

    has_prev = me > 0
    has_next = me < index_count - 1
    prev_place = place(lax.max(me - 1, 0))
    next_place = place(lax.min(me + 1, index_count - 1))

    def remote(source, target, send, recv, where):
        return pltpu.make_async_remote_copy(
            src_ref=source,
            dst_ref=target,
            send_sem=send,
            recv_sem=recv,
            device_id=where,
            device_id_type=MESH,
        )

    halo_next = remote(
        masked.at[pl.ds(pairs - edge, edge)], halo.at[0], halo_send.at[0], halo_recv.at[0], next_place
    )
    halo_prev = remote(masked.at[pl.ds(0, edge)], halo.at[1], halo_send.at[1], halo_recv.at[1], prev_place)
    win_next = remote(own, arrived.at[0], win_send.at[0], win_recv.at[0], next_place)
    win_prev = remote(own, arrived.at[1], win_send.at[1], win_recv.at[1], prev_place)

    def tail_copy(step):
        peer = other(step)
        return remote(
            stage.at[pl.ds(peer * cap, cap)],
            tail_in.at[pl.ds(me * cap, cap)],
            tail_send.at[step],
            tail_recv.at[step],
            place(peer),
        )

    def up_copy(step):
        return remote(
            up_own,
            up_in.at[lvl],
            up_send.at[step],
            up_recv.at[step],
            {"lvl": lax.rem(lvl + step, lvl_count)},
        )

    lanes = lax.broadcasted_iota(jnp.int32, (columns, wide), 1)

    def live(pair):
        first = counts[2 * pair]
        second = counts[2 * pair + 1] + points
        return (lanes < first) | ((lanes >= points) & (lanes < second))

    def spread(pair_block, target, at):
        turned = pair_block.T
        target[at] = turned[:points]
        target[at + 1] = turned[points:]

    loads[0].wait()
    loads[1].wait()

    for pair in range(pairs):
        block = charges[:, pair * wide : (pair + 1) * wide]
        masked[pair] = jnp.where(live(pair), block.astype(jnp.float32), 0.0).astype(jnp.bfloat16)

    loads[2].wait()

    for pair in range(pairs):
        block = masked[pair]
        first = nn(block[:, :points], basis[2 * pair])
        second = nn(block[:, points:], basis[2 * pair + 1])
        own[pair] = packed([first, second]).astype(jnp.bfloat16)
        for half, value in enumerate((first, second)):
            value = value.astype(jnp.bfloat16)
            own_flat[2 * pair + half] = packed([value[: columns // 2], value[columns // 2 :]])

    pl.semaphore_wait(barrier, index_count - 1)

    @pl.when(has_next)
    def _():
        halo_next.start()
        win_next.start()

    @pl.when(has_prev)
    def _():
        halo_prev.start()
        win_prev.start()

    loads[4].wait()
    sums = []
    for parent in range(parents):
        total = None
        for k in range(FAMILY // 2):
            pair = parent * (FAMILY // 2) + k
            block = own[pair]
            term = nn(block[:, :rank], transfer[2 * pair]) + nn(block[:, rank:], transfer[2 * pair + 1])
            total = term if total is None else total + term
        sums.append(total)
    for half in range(parents // 2):
        value = packed(sums[2 * half : 2 * half + 2]).astype(jnp.bfloat16)
        up_own[half] = value
        up_in[lvl, half] = value

    @pl.loop(1, lvl_count)
    def _(step):
        up_copy(step).start()

    loads[3].wait()

    @pl.loop(1, index_count)
    def _(step):
        peer = other(step)
        for j in range(cap):
            stage[peer * cap + j] = own_flat[rows[0, j, peer]]
        tail_copy(step).start()

    for j in range(cap):
        tail_in[me * cap + j] = own_flat[rows[0, j, me]]

    for pair in range(pairs):
        spread(masked[pair], cells, cell_home + 2 * pair)
        spread(own[pair], window, win_home + 2 * pair)

    loads[5].wait()
    loads[6].wait()

    @pl.when(has_prev)
    def _():
        halo_next.wait_recv()
        for pair in range(edge):
            spread(halo[0, pair], cells, cell_away + leaf_dev - HALO + 2 * pair)

    @pl.when(has_next)
    def _():
        halo_prev.wait_recv()
        for pair in range(edge):
            spread(halo[1, pair], cells, cell_away + 2 * pair)

    @pl.loop(0, leaf_dev)
    def _(leaf):
        for k in range(near_even // 2):
            near_packed[leaf, :, k * wide : (k + 1) * wide] = packed([near[leaf, 2 * k], near[leaf, 2 * k + 1]])

    @pl.loop(0, pairs)
    def _(pair):
        for half in range(2):
            leaf = 2 * pair + half
            found = [cells[near_list[leaf, k] & (cell_ring - 1)] for k in range(near_count)]
            total = nn(near_packed[leaf], stacked(found[:near_even]))
            for k in range(near_even, near_count):
                total = total + nn(near[leaf, k], found[k])
            near_sum[leaf] = total

    for i in (7, 8, 9, 10):
        loads[i].wait()

    @pl.loop(0, leaf_dev)
    def _(leaf):
        for k in range(far_count // 2):
            far_packed[leaf, :, k * wide : (k + 1) * wide] = packed([far[leaf, 2 * k], far[leaf, 2 * k + 1]])

    @pl.loop(1, lvl_count)
    def _(step):
        up_copy(step).wait_recv()

    for peer in range(lvl_count):
        for half in range(parents // 2):
            spread(up_in[peer, half], up_all, peer * parents + 2 * half)

    for parent in range(parents):
        total = None
        for k in range(group):
            term = nn(coupling[parent, k], up_all[k])
            total = term if total is None else total + term
        coarse[parent] = total.astype(jnp.bfloat16)

    @pl.loop(1, index_count)
    def _(step):
        tail_copy(step).wait_recv()

    @pl.loop(0, index_count * cap)
    def _(slot):
        turned = tail_in[slot].T
        tail[slot] = packed([turned[:rank], turned[rank:]])

    @pl.when(has_prev)
    def _():
        win_next.wait_recv()
        for pair in range(pairs):
            spread(arrived[0, pair], window, win_prev_home + 2 * pair)

    @pl.when(has_next)
    def _():
        win_prev.wait_recv()
        for pair in range(pairs):
            spread(arrived[1, pair], window, win_next_home + 2 * pair)

    @pl.loop(0, pairs)
    def _(pair):
        parts = []
        for half in range(2):
            leaf = 2 * pair + half
            found = [window[far_list[leaf, k] & (win_ring - 1)] for k in range(win_count)]
            found += [tail[far_slot[k, leaf]] for k in range(far_count - win_count)]
            total = nn(transfer[leaf], coarse[lax.div(pair, FAMILY // 2)])
            total = total + nn(far_packed[leaf], stacked(found))
            parts.append(near_sum[leaf] + nn(basis[leaf], total.astype(jnp.bfloat16)))
        total = jnp.where(live(pair), stacked(parts).T, 0.0)
        out_ref[:, pl.ds(pl.multiple_of(pair * wide, wide), wide)] = total.astype(jnp.bfloat16)

    @pl.when(has_next)
    def _():
        halo_next.wait_send()
        win_next.wait_send()

    @pl.when(has_prev)
    def _():
        halo_prev.wait_send()
        win_prev.wait_send()

    @pl.loop(1, index_count)
    def _(step):
        tail_copy(step).wait_send()

    @pl.loop(1, lvl_count)
    def _(step):
        up_copy(step).wait_send()


def on_device(
    lvl_count,
    index_count,
    charges,
    counts,
    basis,
    transfer,
    far_coupling,
    far_list,
    far_slot,
    send_rows,
    coarse_coupling,
    near_blocks,
    near_list,
):
    columns = charges.shape[0]
    leaf_dev, points, rank = basis.shape
    parents, group = coarse_coupling.shape[:2]
    cap = send_rows.shape[2]
    far_slot = far_slot.T
    send_rows = send_rows.transpose(0, 2, 1)
    half = jnp.bfloat16

    pairs = leaf_dev // 2
    far_wide = far_coupling.shape[1] * rank
    near_wide = near_blocks.shape[1] // 2 * 2 * points

    def turned(count):
        return pltpu.VMEM((count, rank, columns), half)

    dma = pltpu.SemaphoreType.DMA
    return pl.pallas_call(
        functools.partial(kernel, lvl_count, index_count),
        out_shape=jax.ShapeDtypeStruct(charges.shape, half),
        in_specs=[pl.BlockSpec(memory_space=pl.ANY)] * 11,
        out_specs=pl.BlockSpec(memory_space=pltpu.VMEM),
        scratch_shapes=[
            pltpu.VMEM(charges.shape, half),
            pltpu.VMEM(basis.shape, half),
            pltpu.VMEM(transfer.shape, half),
            pltpu.VMEM(far_coupling.shape, half),
            pltpu.VMEM(coarse_coupling.shape, half),
            pltpu.VMEM(near_blocks.shape, half),
            pltpu.SMEM(counts.shape, jnp.int32),
            pltpu.SMEM(far_list.shape, jnp.int32),
            pltpu.SMEM(far_slot.shape, jnp.int32),
            pltpu.SMEM(send_rows.shape, jnp.int32),
            pltpu.SMEM(near_list.shape, jnp.int32),
            pltpu.VMEM((pairs, columns, 2 * points), half),
            pltpu.VMEM((2, HALO // 2, columns, 2 * points), half),
            pltpu.VMEM((pairs, columns, 2 * rank), half),
            pltpu.VMEM((leaf_dev, columns // 2, 2 * rank), half),
            pltpu.VMEM((index_count * cap, columns // 2, 2 * rank), half),
            pltpu.VMEM((2, pairs, columns, 2 * rank), half),
            pltpu.VMEM((index_count * cap, columns // 2, 2 * rank), half),
            pltpu.VMEM((parents // 2, columns, 2 * rank), half),
            pltpu.VMEM((lvl_count, parents // 2, columns, 2 * rank), half),
            turned(2 * leaf_dev),
            turned(4 * leaf_dev),
            turned(index_count * cap),
            turned(group),
            turned(parents),
            pltpu.VMEM((leaf_dev, rank, far_wide), half),
            pltpu.VMEM((leaf_dev, points, near_wide), half),
            pltpu.VMEM((leaf_dev, points, columns), jnp.float32),
            dma((11,)),
            dma((2,)),
            dma((2,)),
            dma((2,)),
            dma((2,)),
            dma((index_count,)),
            dma((index_count,)),
            dma((lvl_count,)),
            dma((lvl_count,)),
        ],
        compiler_params=pltpu.CompilerParams(
            collective_id=0, has_side_effects=True, vmem_limit_bytes=63 * 1024 * 1024
        ),
    )(
        charges,
        counts,
        basis,
        transfer,
        far_coupling,
        far_list,
        far_slot,
        send_rows,
        coarse_coupling,
        near_blocks,
        near_list,
    )


def solution(mesh):
    every = ("grp", "box", "lvl")
    placed = (
        P("rhs", every),
        P(every),
        P(every, None, None),
        P(every, None, None),
        P(every, None, None, None),
        P(every, None),
        P(every, None),
        P(every, None, None),
        P(every, None, None, None),
        P(every, None, None, None),
        P(every, None),
    )
    lvl_count = mesh.shape["lvl"]
    return jax.shard_map(
        functools.partial(on_device, lvl_count, lvl_count * mesh.shape["box"]),
        mesh=mesh,
        in_specs=placed,
        out_specs=P("rhs", every),
        check_vma=False,
    )
```

time: 33.5 us -> 21.7 us (0.65)
  the two profiles are of different devices: /device:TPU:7 before, /device:TPU:0 now
where the time goes in v2:
time: 21.7 us; the launch traced here: 21.5 us
  Pallas kernels  20 us (92%)
  local copies, waits for them, and re-layouts  1.47 us (7%)
    pallas_call x1, Pallas kernels, on_device(): pl.pallas_call(functools.partial(kernel, lvl_count, index_count), out_sha...  20 us
    unnamed x1, local copies, waits for them, and re-layouts  1.47 us

profile of v2, /device:TPU:0, one launch (start us, length us, event | category | flops | bytes accessed | tf_op | source)
XLA Modules:
  0.0 21.5 jit_solution(16249837529331358321)
XLA Ops:
  0.0 20.0 %shard_map.109 = bf16[32,1024]{1,0:T(8,128)(2,1)} custom-call(bf16[32,1024]{1,0:T(8,128)(2,1)} %charges_hbm.1, s32[16]{0:T(128)} %counts_hbm.1, bf16[16,64,64]{2,1,0:T(8,128)(2,1)} %basis_hbm.1, bf16[16,64,64]{2,1,0:T(8,128)(2,1)} %transfer_hbm.1, bf16[16,20,64,64]{3,2,1,0:T(8,128)(2,1)} %far_hbm.1, s32[16,12]{1,0:T(8,128)} %far_list_hbm.1, ...), custom_call_target="tpu_custom_call" | custom-call | tf_op jit(solution)/shard_map/pallas_call | solution.py:390
  20.0 1.5 %copy.13 = bf16[32,1024]{1,0:T(8,128)(2,1)} copy(bf16[32,1024]{1,0:T(8,128)(2,1)} %shard_map.109) | data formatting | bytes 131072

commit v3 on v2

--- a/solution.py
+++ b/solution.py
@@ -64,8 +64,6 @@
     tail,
     up_all,
     coarse,
-    far_packed,
-    near_packed,
     near_sum,
     load_sem,
     halo_send,
@@ -265,28 +263,18 @@
         for pair in range(edge):
             spread(halo[1, pair], cells, cell_away + 2 * pair)
 
-    @pl.loop(0, leaf_dev)
-    def _(leaf):
-        for k in range(near_even // 2):
-            near_packed[leaf, :, k * wide : (k + 1) * wide] = packed([near[leaf, 2 * k], near[leaf, 2 * k + 1]])
-
-    @pl.loop(0, pairs)
+    @pl.loop(0, pairs, unroll=8)
     def _(pair):
         for half in range(2):
             leaf = 2 * pair + half
             found = [cells[near_list[leaf, k] & (cell_ring - 1)] for k in range(near_count)]
-            total = nn(near_packed[leaf], stacked(found[:near_even]))
+            total = nn(packed([near[leaf, k] for k in range(near_even)]), stacked(found[:near_even]))
             for k in range(near_even, near_count):
                 total = total + nn(near[leaf, k], found[k])
             near_sum[leaf] = total
 
     for i in (7, 8, 9, 10):
         loads[i].wait()
-
-    @pl.loop(0, leaf_dev)
-    def _(leaf):
-        for k in range(far_count // 2):
-            far_packed[leaf, :, k * wide : (k + 1) * wide] = packed([far[leaf, 2 * k], far[leaf, 2 * k + 1]])
 
     @pl.loop(1, lvl_count)
     def _(step):
@@ -307,7 +295,7 @@
     def _(step):
         tail_copy(step).wait_recv()
 
-    @pl.loop(0, index_count * cap)
+    @pl.loop(0, index_count * cap, unroll=4)
     def _(slot):
         turned = tail_in[slot].T
         tail[slot] = packed([turned[:rank], turned[rank:]])
@@ -324,7 +312,7 @@
         for pair in range(pairs):
             spread(arrived[1, pair], window, win_next_home + 2 * pair)
 
-    @pl.loop(0, pairs)
+    @pl.loop(0, pairs, unroll=8)
     def _(pair):
         parts = []
         for half in range(2):
@@ -332,7 +320,7 @@
             found = [window[far_list[leaf, k] & (win_ring - 1)] for k in range(win_count)]
             found += [tail[far_slot[k, leaf]] for k in range(far_count - win_count)]
             total = nn(transfer[leaf], coarse[lax.div(pair, FAMILY // 2)])
-            total = total + nn(far_packed[leaf], stacked(found))
+            total = total + nn(packed([far[leaf, k] for k in range(far_count)]), stacked(found))
             parts.append(near_sum[leaf] + nn(basis[leaf], total.astype(jnp.bfloat16)))
         total = jnp.where(live(pair), stacked(parts).T, 0.0)
         out_ref[:, pl.ds(pl.multiple_of(pair * wide, wide), wide)] = total.astype(jnp.bfloat16)
@@ -380,8 +368,6 @@
     half = jnp.bfloat16
 
     pairs = leaf_dev // 2
-    far_wide = far_coupling.shape[1] * rank
-    near_wide = near_blocks.shape[1] // 2 * 2 * points
 
     def turned(count):
         return pltpu.VMEM((count, rank, columns), half)
@@ -418,8 +404,6 @@
             turned(index_count * cap),
             turned(group),
             turned(parents),
-            pltpu.VMEM((leaf_dev, rank, far_wide), half),
-            pltpu.VMEM((leaf_dev, points, near_wide), half),
             pltpu.VMEM((leaf_dev, points, columns), jnp.float32),
             dma((11,)),
             dma((2,)),

time: 21.7 us -> 16.2 us (0.75)
  the two profiles are of different devices: /device:TPU:0 before, /device:TPU:7 now
where the time goes in v3:
time: 16.2 us; the launch traced here: 16 us
  Pallas kernels  14.5 us (90%)
  local copies, waits for them, and re-layouts  1.47 us (9%)
    pallas_call x1, Pallas kernels, on_device(): pl.pallas_call(functools.partial(kernel, lvl_count, index_count), out_sha...  14.5 us
    unnamed x1, local copies, waits for them, and re-layouts  1.47 us

profile of v3, /device:TPU:7, one launch (start us, length us, event | category | flops | bytes accessed | tf_op | source)
XLA Modules:
  0.0 16.0 jit_solution(3971579994855947405)
XLA Ops:
  0.0 14.5 %shard_map.109 = bf16[32,1024]{1,0:T(8,128)(2,1)} custom-call(bf16[32,1024]{1,0:T(8,128)(2,1)} %charges_hbm.1, s32[16]{0:T(128)} %counts_hbm.1, bf16[16,64,64]{2,1,0:T(8,128)(2,1)} %basis_hbm.1, bf16[16,64,64]{2,1,0:T(8,128)(2,1)} %transfer_hbm.1, bf16[16,20,64,64]{3,2,1,0:T(8,128)(2,1)} %far_hbm.1, s32[16,12]{1,0:T(8,128)} %far_list_hbm.1, ...), custom_call_target="tpu_custom_call" | custom-call | tf_op jit(solution)/shard_map/pallas_call | solution.py:376
  14.5 1.5 %copy.13 = bf16[32,1024]{1,0:T(8,128)(2,1)} copy(bf16[32,1024]{1,0:T(8,128)(2,1)} %shard_map.109) | data formatting | bytes 131072

commit v4 on v3

--- a/solution.py
+++ b/solution.py
@@ -251,20 +251,7 @@
     loads[5].wait()
     loads[6].wait()
 
-    @pl.when(has_prev)
-    def _():
-        halo_next.wait_recv()
-        for pair in range(edge):
-            spread(halo[0, pair], cells, cell_away + leaf_dev - HALO + 2 * pair)
-
-    @pl.when(has_next)
-    def _():
-        halo_prev.wait_recv()
-        for pair in range(edge):
-            spread(halo[1, pair], cells, cell_away + 2 * pair)
-
-    @pl.loop(0, pairs, unroll=8)
-    def _(pair):
+    def near_pair(pair):
         for half in range(2):
             leaf = 2 * pair + half
             found = [cells[near_list[leaf, k] & (cell_ring - 1)] for k in range(near_count)]
@@ -272,6 +259,24 @@
             for k in range(near_even, near_count):
                 total = total + nn(near[leaf, k], found[k])
             near_sum[leaf] = total
+
+    for pair in range(edge, pairs - edge):
+        near_pair(pair)
+
+    @pl.when(has_prev)
+    def _():
+        halo_next.wait_recv()
+        for pair in range(edge):
+            spread(halo[0, pair], cells, cell_away + leaf_dev - HALO + 2 * pair)
+
+    @pl.when(has_next)
+    def _():
+        halo_prev.wait_recv()
+        for pair in range(edge):
+            spread(halo[1, pair], cells, cell_away + 2 * pair)
+
+    for pair in (*range(edge), *range(pairs - edge, pairs)):
+        near_pair(pair)
 
     for i in (7, 8, 9, 10):
         loads[i].wait()

time: 16.2 us -> 16.2 us (level)
  no operation moved by 1% of the time
where the time goes in v4:
time: 16.2 us; the launch traced here: 16 us
  Pallas kernels  14.5 us (90%)
  local copies, waits for them, and re-layouts  1.47 us (9%)
    pallas_call x1, Pallas kernels, on_device(): pl.pallas_call(functools.partial(kernel, lvl_count, index_count), out_sha...  14.5 us
    unnamed x1, local copies, waits for them, and re-layouts  1.47 us

profile of v4, /device:TPU:7, one launch (start us, length us, event | category | flops | bytes accessed | tf_op | source)
XLA Modules:
  0.0 16.0 jit_solution(5210200748125556836)
XLA Ops:
  0.0 14.5 %shard_map.109 = bf16[32,1024]{1,0:T(8,128)(2,1)} custom-call(bf16[32,1024]{1,0:T(8,128)(2,1)} %charges_hbm.1, s32[16]{0:T(128)} %counts_hbm.1, bf16[16,64,64]{2,1,0:T(8,128)(2,1)} %basis_hbm.1, bf16[16,64,64]{2,1,0:T(8,128)(2,1)} %transfer_hbm.1, bf16[16,20,64,64]{3,2,1,0:T(8,128)(2,1)} %far_hbm.1, s32[16,12]{1,0:T(8,128)} %far_list_hbm.1, ...), custom_call_target="tpu_custom_call" | custom-call | tf_op jit(solution)/shard_map/pallas_call | solution.py:381
  14.5 1.5 %copy.13 = bf16[32,1024]{1,0:T(8,128)(2,1)} copy(bf16[32,1024]{1,0:T(8,128)(2,1)} %shard_map.109) | data formatting | bytes 131072
